TPU v7x, 512 devices: a whole 4x4x16 slice. The times are simulated.
512 devices in a mesh: seg: 16 (over z_hi, x), coil: 32 (over y, z_lo, core).
Axes of the slice: x: 4, y: 4, z: 16 (z_hi: 4, z_lo: 4; z = z_hi * 4 + z_lo), core: 2. Of those that a mesh axis runs over, the one named last changes fastest.
Arguments:
- image_estimate: bfloat16 [1, 384, 768], replicated, may hold values from -6 to 6
- coil_maps: bfloat16 [32, 384, 768], P('coil'), may hold values from -3 to 3
- field_map: float32 [384, 384], replicated, may hold values from -3 to 3
- interp_rows: bfloat16 [1, 256, 384], replicated, may hold values from -0.3125 to 0.3125
- interp_cols: bfloat16 [1, 128, 384], replicated, may hold values from -0.3125 to 0.3125
- measured: bfloat16 [32, 1, 256, 256], P('coil'), may hold values from -6 to 6
- sample_time: int32 [1, 256], replicated, may hold values from 0 to 60
- sample_count: int32 [1], replicated, may hold values from 128 to 256
Outputs:
- gradient: float32 [1, 384, 768], P(None, 'coil', 'seg')
- residual: float32 [32, 1, 256, 256], P('coil', None, 'seg')
Inputs may be any that keep to these rules, and one draw needn't show every extreme that they name: sample_time counts the sample clock, 4 steps to a segment. Rows below sample_count[p] of partition p are acquired.
All inputs are finite; a program needn't handle non-finite values.
Results may differ from a plain program's by a relative error of at most 0.017.
Values sent between devices are 32-bit elements; how exact they have to be, the bound alone decides.
A program may use at most 64 MiB of HBM per device.

v0:
```python
import math
import jax
import jax.numpy as jnp
from jax import lax
from jax.sharding import PartitionSpec as P

SUBSTEPS = 4


def dft_tables(length):
    indices = jnp.arange(length, dtype=jnp.int32)
    wrapped = indices[:, None] * indices[None, :] % length
    angles = wrapped.astype(jnp.float32) * (2.0 * math.pi / length)
    factor = 1.0 / math.sqrt(length)
    return (jnp.cos(angles) * factor, jnp.sin(angles) * factor)


def shards(
    image_estimate,
    coil_maps,
    field_map,
    interp_rows,
    interp_cols,
    measured,
    sample_time,
    sample_count,
):
    segment = lax.axis_index("seg")
    seg_total = lax.axis_size("seg")
    coil_total = lax.axis_size("coil")
    pixels = field_map.shape[0]
    row_total = interp_rows.shape[1]
    col_total = interp_cols.shape[1]
    own_rows = row_total // seg_total
    start_row = segment * own_rows
    cosine, sine = dft_tables(pixels)
    stacked_table = jnp.concatenate([cosine, sine], axis=0).astype(jnp.bfloat16)
    forward_right = jnp.concatenate(
        [jnp.concatenate([cosine, -sine], 1), jnp.concatenate([sine, cosine], 1)], 0
    ).astype(jnp.bfloat16)
    inverse_right = jnp.concatenate(
        [jnp.concatenate([cosine, sine], 1), jnp.concatenate([-sine, cosine], 1)], 0
    ).astype(jnp.bfloat16)
    offset = segment.astype(jnp.float32) - 0.5 * (seg_total - 1)
    angles = field_map * offset
    phase_re = jnp.cos(angles)
    phase_im = jnp.sin(angles)
    maps = coil_maps[0].astype(jnp.float32)
    sens_re = maps[:, :pixels]
    sens_im = maps[:, pixels:]
    comb_re = sens_re * phase_re - sens_im * phase_im
    comb_im = sens_re * phase_im + sens_im * phase_re
    factor = coil_total ** (-0.5)
    row_ids = jnp.arange(row_total, dtype=jnp.int32)
    current = image_estimate[0].astype(jnp.float32)
    cur_re = current[:, :pixels]
    cur_im = current[:, pixels:]
    weighted = jnp.concatenate(
        [cur_re * comb_re - cur_im * comb_im, cur_re * comb_im + cur_im * comb_re], 1
    ).astype(jnp.bfloat16)
    products = jnp.dot(stacked_table, weighted, preferred_element_type=jnp.float32)
    cos_part = products[:pixels]
    sin_part = products[pixels:]
    rows_ft = jnp.concatenate(
        [cos_part[:, :pixels] + sin_part[:, pixels:], cos_part[:, pixels:] - sin_part[:, :pixels]],
        1,
    ).astype(jnp.bfloat16)
    kspace = jnp.dot(rows_ft, forward_right, preferred_element_type=jnp.float32).astype(
        jnp.bfloat16
    )
    picked = jnp.dot(interp_rows[0], kspace, preferred_element_type=jnp.float32).astype(
        jnp.bfloat16
    )
    sampled = jnp.einsum(
        "mrn,kn->mrk",
        picked.reshape(row_total, 2, pixels),
        interp_cols[0],
        preferred_element_type=jnp.float32,
    ).reshape(row_total, 2 * col_total)
    sample_steps = sample_time[0].astype(jnp.float32)
    weights = jnp.maximum(
        0.0, 1.0 - jnp.abs(sample_steps - (segment * SUBSTEPS).astype(jnp.float32)) / SUBSTEPS
    )
    partial_sum = weights[:, None] * sampled
    sampled_mask = (row_ids < sample_count[0]).astype(jnp.float32)[:, None]
    data_rows = measured[0, 0].astype(jnp.float32)
    totals = lax.psum(partial_sum, "seg")
    misfit = sampled_mask * (totals - data_rows)
    misfit_own = lax.dynamic_slice_in_dim(misfit, start_row, own_rows, 0)
    back_weighted = (weights[:, None] * misfit).astype(jnp.bfloat16)
    spread = lax.dot_general(
        interp_rows[0], back_weighted, (((0,), (0,)), ((), ())), preferred_element_type=jnp.float32
    ).astype(jnp.bfloat16)
    gridded = (
        jnp.einsum(
            "nrk,kj->nrj",
            spread.reshape(pixels, 2, col_total),
            interp_cols[0],
            preferred_element_type=jnp.float32,
        )
        .reshape(pixels, 2 * pixels)
        .astype(jnp.bfloat16)
    )
    back_products = jnp.dot(stacked_table, gridded, preferred_element_type=jnp.float32)
    cos_back = back_products[:pixels]
    sin_back = back_products[pixels:]
    back_rows = jnp.concatenate(
        [cos_back[:, :pixels] - sin_back[:, pixels:], cos_back[:, pixels:] + sin_back[:, :pixels]],
        1,
    ).astype(jnp.bfloat16)
    back_image = jnp.dot(back_rows, inverse_right, preferred_element_type=jnp.float32)
    image_re = back_image[:, :pixels]
    image_im = back_image[:, pixels:]
    image_term = factor * jnp.concatenate(
        [comb_re * image_re + comb_im * image_im, comb_re * image_im - comb_im * image_re], 1
    )
    across = lax.psum_scatter(image_term, "coil", scatter_dimension=0, tiled=True)
    reduced = lax.psum_scatter(across, "seg", scatter_dimension=1, tiled=True)
    gradients = [reduced]
    residuals = [misfit_own]
    gradient = jnp.stack(gradients, axis=0)
    residual = jnp.stack(residuals, axis=0)[None]
    return (gradient, residual)


def solution(mesh):
    in_specs = (P(), P("coil", None, None), P(), P(), P(), P("coil", None, None, None), P(), P())
    out_specs = (P(None, "coil", "seg"), P("coil", None, "seg", None))
    return jax.shard_map(shards, mesh=mesh, in_specs=in_specs, out_specs=out_specs, check_vma=False)
```

profile of v0, /device:TPU:8, one launch (start us, length us, event | category | flops | bytes accessed | tf_op | source)
XLA Modules:
  0.0 456.2 jit_solution(10161998638075263033)
XLA Ops:
  7.2 0.0 copy-start
  7.2 0.0 copy-start.2
  7.2 0.0 all-reduce.4.cloned.1.call-start
  7.2 3.0 negate_convert_fusion
  10.2 2.6 multiply_convert_fusion
  12.8 0.0 copy-done.2
  12.8 0.0 copy-start.1
  12.8 1.3 bitcast_convert_fusion
  14.1 0.0 copy-done.1
  14.1 2.4 subtract_convert_fusion
  16.5 0.2 add_convert_fusion
  16.7 0.8 fusion.21
  17.5 0.1 fusion.20
  17.6 0.0 copy-done
  17.6 0.0 copy-start.3
  17.6 2.3 fusion.2
  19.9 0.0 copy-start.6
  19.9 0.0 copy-start.5
  19.9 0.0 copy-done.3
  20.0 0.2 fusion.44
  20.2 0.1 copy.16
  20.3 0.3 copy-done.6
  20.6 0.8 broadcast_multiply_fusion
  21.4 0.0 all-reduce.4.cloned.1.call-update
  21.4 0.0 reduce-scatter.6.cloned.1.call-start
  22.2 205.4 %all-reduce.4.cloned.1.call-done = f32[256,256]{1,0:T(8,128)} async-done(((f32[256,256]{1,0:T(8,128)}), f32[256,256]{1,0:T(8,128)}) %all-reduce.4.cloned.1.call-update) | async-done | bytes 262160 | tf_op jit(solution)/shard_map/psum | solution.py:87
  227.6 0.0 copy-done.5
  227.6 1.0 fusion.39
  228.7 0.3 convolution_convert_fusion.2
  229.0 0.4 convolution_convert_fusion
  229.4 0.8 fusion.38
  230.2 0.0 copy-start.4
  230.2 0.1 fusion.18
  230.3 0.8 copy-done.4
  231.1 0.7 fusion.7
  231.8 0.2 multiply_add_fusion
  232.0 0.1 maximum_multiply_fusion
  232.1 67.6 %fusion = f32[16,768]{1,0:T(8,128)S(1)} fusion(f32[384,768]{1,0:T(8,128)S(1)} %maximum_multiply_fusion), kind=kCustom, calls=%all-reduce-scatter | all-reduce-scatter fusion | flops 393217 | bytes 1230848
  299.8 1.9 collective-permute-start.6
  301.7 1.9 collective-permute-start.5
  303.6 8.6 %collective-permute-start.7 = (f32[12,768]{1,0:T(8,128)S(1)}, f32[12,768]{1,0:T(8,128)S(1)}, u32[]{:S(2)}, u32[]{:S(2)}) collective-permute-start(f32[12,768]{1,0:T(8,128)S(1)} %slice.82), channel_id=1, source_target_pairs={{0,8},{1,9},{2,10},{3,11},{4,12},{5,13},{6,14},{7,15},{8,16},{9,17... | collective-permute-start | bytes 110600
  312.2 1.9 collective-permute-start.4
  314.2 8.2 %collective-permute-start.3 = (f32[16,768]{1,0:T(8,128)S(1)}, f32[16,768]{1,0:T(8,128)S(1)}, u32[]{:S(2)}, u32[]{:S(2)}) collective-permute-start(f32[16,768]{1,0:T(8,128)S(1)} %fusion), channel_id=1, source_target_pairs={{0,4},{1,5},{2,6},{3,7},{4,8},{5,9},{6,10},{7,11},{8,12},{9,13},{1... | collective-permute-start | bytes 147464
  322.4 0.0 collective-permute-done.7
  322.4 1.9 collective-permute-start.2
  324.3 0.0 collective-permute-done.6
  324.3 3.4 collective-permute-start.1
  327.7 0.0 collective-permute-done.5
  327.7 2.9 collective-permute-start
  330.7 1.3 dynamic-slice.4
  332.6 0.0 collective-permute-done.4
  332.6 0.0 collective-permute-done.3
  332.6 0.0 collective-permute-done.2
  332.6 1.3 collective-permute-done.1
  333.9 2.0 collective-permute-done
  335.8 1.0 concatenate.54
  336.9 0.9 copy.24
  337.8 0.0 reduce-scatter.6.cloned.1.call-update
  337.8 0.6 dynamic-slice_bitcast_fusion
  338.5 109.4 %reduce-scatter.6.cloned.1.call-done = f32[48,12]{1,0:T(8,128)} async-done(((f32[768,12]{1,0:T(8,128)}), f32[48,12]{1,0:T(8,128)}) %reduce-scatter.6.cloned.1.call-update) | async-done | bytes 2320
  447.9 0.8 copy.25
  448.7 0.6 copy.19
  (4 shorter events, 0.0 us)
Async XLA Ops:
  7.2 10.5 %copy-start = (bf16[1,256,384]{2,1,0:T(8,128)(2,1)S(1)}, bf16[1,256,384]{2,1,0:T(8,128)(2,1)}, u32[]{:S(2)}) copy-start(bf16[1,256,384]{2,1,0:T(8,128)(2,1)} %param.11) | copy-start | bytes 589828
  7.2 5.6 %copy-start.2 = (bf16[1,384,768]{2,1,0:T(8,128)(2,1)S(1)}, bf16[1,384,768]{2,1,0:T(8,128)(2,1)}, u32[]{:S(2)}) copy-start(bf16[1,384,768]{2,1,0:T(8,128)(2,1)} %param.8) | copy-start | bytes 1769476
  7.2 220.4 %all-reduce.4.cloned.1.call-start = ((), (), s32[]{:S(2)}) async-start(), calls=%async_computation.1 | async-start | bytes 524288 | tf_op jit(solution)/shard_map/psum | solution.py:87
  12.8 1.3 copy-start.1
  17.6 2.3 copy-start.3
  19.9 0.7 copy-start.6
  19.9 207.7 %copy-start.5 = (bf16[1,1,256,256]{3,2,1,0:T(8,128)(2,1)S(1)}, bf16[1,1,256,256]{3,2,1,0:T(8,128)(2,1)}, u32[]{:S(2)}) copy-start(bf16[1,1,256,256]{3,2,1,0:T(8,128)(2,1)} %param.13) | copy-start | bytes 393220
  21.4 426.5 %reduce-scatter.6.cloned.1.call-start = ((), (), s32[]{:S(2)}) async-start(), calls=%async_computation.2 | async-start | bytes 417792
  230.2 1.0 copy-start.4
  299.8 24.6 %collective-permute-start.6 = (f32[16,768]{1,0:T(8,128)S(1)}, f32[16,768]{1,0:T(8,128)S(1)}, u32[]{:S(2)}, u32[]{:S(2)}) collective-permute-start(f32[16,768]{1,0:T(8,128)S(1)} %fusion), channel_id=1, source_target_pairs={{0,7},{1,8},{2,9},{3,10},{4,11},{5,12},{6,13},{7,14},{8,15},{9,16}... | collective-permute-start | bytes 147464
  301.7 26.0 %collective-permute-start.5 = (f32[16,768]{1,0:T(8,128)S(1)}, f32[16,768]{1,0:T(8,128)S(1)}, u32[]{:S(2)}, u32[]{:S(2)}) collective-permute-start(f32[16,768]{1,0:T(8,128)S(1)} %fusion), channel_id=1, source_target_pairs={{0,6},{1,7},{2,8},{3,9},{4,10},{5,11},{6,12},{7,13},{8,14},{9,15},... | collective-permute-start | bytes 147464
  303.6 18.7 %collective-permute-start.7 = (f32[12,768]{1,0:T(8,128)S(1)}, f32[12,768]{1,0:T(8,128)S(1)}, u32[]{:S(2)}, u32[]{:S(2)}) collective-permute-start(f32[12,768]{1,0:T(8,128)S(1)} %slice.82), channel_id=1, source_target_pairs={{0,8},{1,9},{2,10},{3,11},{4,12},{5,13},{6,14},{7,15},{8,16},{9,17... | collective-permute-start | bytes 110600
  312.2 20.3 %collective-permute-start.4 = (f32[16,768]{1,0:T(8,128)S(1)}, f32[16,768]{1,0:T(8,128)S(1)}, u32[]{:S(2)}, u32[]{:S(2)}) collective-permute-start(f32[16,768]{1,0:T(8,128)S(1)} %fusion), channel_id=1, source_target_pairs={{0,5},{1,6},{2,7},{3,8},{4,9},{5,10},{6,11},{7,12},{8,13},{9,14},{... | collective-permute-start | bytes 147464
  314.2 18.4 %collective-permute-start.3 = (f32[16,768]{1,0:T(8,128)S(1)}, f32[16,768]{1,0:T(8,128)S(1)}, u32[]{:S(2)}, u32[]{:S(2)}) collective-permute-start(f32[16,768]{1,0:T(8,128)S(1)} %fusion), channel_id=1, source_target_pairs={{0,4},{1,5},{2,6},{3,7},{4,8},{5,9},{6,10},{7,11},{8,12},{9,13},{1... | collective-permute-start | bytes 147464
  322.4 10.2 %collective-permute-start.2 = (f32[16,768]{1,0:T(8,128)S(1)}, f32[16,768]{1,0:T(8,128)S(1)}, u32[]{:S(2)}, u32[]{:S(2)}) collective-permute-start(f32[16,768]{1,0:T(8,128)S(1)} %fusion), channel_id=1, source_target_pairs={{0,3},{1,4},{2,5},{3,6},{4,7},{5,8},{6,9},{7,10},{8,11},{9,12},{10... | collective-permute-start | bytes 147464
  324.3 9.5 %collective-permute-start.1 = (f32[16,768]{1,0:T(8,128)S(1)}, f32[16,768]{1,0:T(8,128)S(1)}, u32[]{:S(2)}, u32[]{:S(2)}) collective-permute-start(f32[16,768]{1,0:T(8,128)S(1)} %fusion), channel_id=1, source_target_pairs={{0,2},{1,3},{2,4},{3,5},{4,6},{5,7},{6,8},{7,9},{8,10},{9,11},{10,... | collective-permute-start | bytes 147464
  327.7 8.1 %collective-permute-start = (f32[16,768]{1,0:T(8,128)S(1)}, f32[16,768]{1,0:T(8,128)S(1)}, u32[]{:S(2)}, u32[]{:S(2)}) collective-permute-start(f32[16,768]{1,0:T(8,128)S(1)} %fusion), channel_id=1, source_target_pairs={{0,1},{1,2},{2,3},{3,4},{4,5},{5,6},{6,7},{7,8},{8,9},{9,10},{10,1... | collective-permute-start | bytes 147464
Sparse Core Ops, SparseCore 0:
  21.6 205.9 all-reduce.3
  338.0 109.8 reduce-scatter.5
where the time goes:
time: 457 us; the launch traced here: 456 us
  waiting for transfers between devices  318 us (70%)
  blocking collectives  67.6 us (15%)
  starting transfers between devices  30.9 us (7%)
  between operations  15.7 us (3%)
  other arithmetic  11.7 us (3%)
  local copies, waits for them, and re-layouts  6.57 us (1%)
  matrix products  5.5 us (1%)
    psum x1, waiting for transfers between devices, shards(): totals = lax.psum(partial_sum, 'seg')  205 us
    unnamed x11, waiting for transfers between devices  113 us
    unnamed x1, blocking collectives  67.6 us
    unnamed x9, starting transfers between devices  30.8 us
  transfers between devices with their start and end apart: 10, of which 4 were waited for; matrix products, arithmetic and copies ran while one was open for 0% of the time, Pallas kernels for 0%

commit v1 on v0

--- a/solution.py
+++ b/solution.py
@@ -84,7 +84,7 @@
     partial_sum = weights[:, None] * sampled
     sampled_mask = (row_ids < sample_count[0]).astype(jnp.float32)[:, None]
     data_rows = measured[0, 0].astype(jnp.float32)
-    totals = lax.psum(partial_sum, "seg")
+    totals = jnp.sum(lax.all_gather(partial_sum, "seg"), axis=0)
     misfit = sampled_mask * (totals - data_rows)
     misfit_own = lax.dynamic_slice_in_dim(misfit, start_row, own_rows, 0)
     back_weighted = (weights[:, None] * misfit).astype(jnp.bfloat16)

time: 457 us -> 384 us (0.84)
  waiting for transfers between devices: 318 us -> 246 us
    psum x1 -> x0, waiting for transfers between devices: 205 us -> none  [shards(): totals = lax.psum(partial_sum, 'seg')]
    all_gather x0 -> x1, waiting for transfers between devices: none -> 138 us  [shards(): totals = jnp.sum(lax.all_gather(partial_sum, 'seg'), axis=0)]
  transfers between devices with their start and end apart: 10 -> 10, of which waited for: 4 -> 5; matrix products, arithmetic and copies ran while one was open for 0% -> 1% of each run, Pallas kernels for 0% -> 0%
where the time goes in v1:
time: 384 us
  waiting for transfers between devices  246 us (64%)
  blocking collectives  66.4 us (17%)
  starting transfers between devices  27.4 us (7%)
  other arithmetic  15.8 us (4%)
  between operations  15.7 us (4%)
  local copies, waits for them, and re-layouts  6.92 us (2%)
  matrix products  5.4 us (1%)
    all_gather x1, waiting for transfers between devices, shards(): totals = jnp.sum(lax.all_gather(partial_sum, 'seg'), axis=0)  138 us
    unnamed x11, waiting for transfers between devices  108 us
    unnamed x1, blocking collectives  66.4 us
    unnamed x9, starting transfers between devices  27.4 us
    another operation x6, other arithmetic  9.78 us
  transfers between devices with their start and end apart: 10, of which 5 were waited for; matrix products, arithmetic and copies ran while one was open for 1% of the time, Pallas kernels for 0%

profile of v1, /device:TPU:8, one launch (start us, length us, event | category | flops | bytes accessed | tf_op | source)
XLA Modules:
  0.0 383.8 jit_solution(2147771669760490195)
XLA Ops:
  7.2 0.0 copy-start
  7.2 0.0 copy-start.1
  7.2 0.0 all-gather.2.cloned.1.call-start
  7.2 2.6 multiply_convert_fusion
  9.8 3.0 negate_convert_fusion
  12.8 0.0 copy-done.1
  12.8 2.3 bitcast_convert_fusion
  15.1 3.9 %subtract_convert_fusion = (bf16[384,384]{1,0:T(8,128)(2,1)S(1)}, f32[384,384]{1,0:T(8,128)S(1)}, f32[384,384]{1,0:T(8,128)S(1)}) fusion(f32[384,768]{1,0:T(8,128)S(1)} %get-tuple-element.17, f32[384,768]{1,0:T(8,128)} %get-tuple-element.18, f32[384,384]{1,0:T(8,128)} %param.10, f32[]{:T(128)S(6)} %sub.45), kind=kLoop, calls=%fused_computation.45 | loop fusion | flops 1622016 | bytes 4423684 | tf_op jit(solution)/shard_map/convert.19
  19.0 0.1 add_convert_fusion
  19.1 0.8 fusion.21
  19.9 0.1 fusion.20
  20.0 0.0 copy-done
  20.1 0.0 copy-start.2
  20.1 2.3 fusion.2
  22.3 0.0 copy-start.5
  22.4 0.0 copy-start.4
  22.4 0.0 copy-done.2
  22.4 0.2 fusion.50
  22.6 0.1 copy.22
  22.8 0.3 copy-done.5
  23.0 0.8 broadcast_multiply_fusion
  23.8 0.0 all-gather.2.cloned.1.call-update
  23.9 0.0 reduce-scatter.6.cloned.1.call-start
  23.9 0.0 copy-done.4
  23.9 0.1 copy.24
  24.7 137.8 %all-gather.2.cloned.1.call-done = f32[16,256,256]{2,1,0:T(8,128)} async-done(((f32[1,256,256]{2,1,0:T(8,128)}), f32[16,256,256]{2,1,0:T(8,128)}) %all-gather.2.cloned.1.call-update) | async-done | bytes 4194320 | tf_op jit(solution)/shard_map/all_gather | solution.py:87
  162.5 2.5 reduce_sum.11
  165.0 0.1 copy.35
  165.2 0.2 convolution_convert_fusion.2
  165.4 0.4 convolution_convert_fusion
  165.8 0.8 fusion.38
  166.6 0.0 copy-start.3
  166.6 0.1 fusion.18
  166.7 0.8 copy-done.3
  167.5 0.7 fusion.7
  168.2 0.2 multiply_add_fusion
  168.4 0.1 maximum_multiply_fusion
  168.5 66.4 %fusion = f32[16,768]{1,0:T(8,128)S(1)} fusion(f32[384,768]{1,0:T(8,128)S(1)} %maximum_multiply_fusion), kind=kCustom, calls=%all-reduce-scatter | all-reduce-scatter fusion | flops 393217 | bytes 1230848
  234.9 1.9 collective-permute-start
  236.8 1.9 collective-permute-start.1
  238.7 3.4 collective-permute-start.7
  242.2 1.9 collective-permute-start.2
  244.1 6.7 %collective-permute-start.3 = (f32[16,768]{1,0:T(8,128)S(1)}, f32[16,768]{1,0:T(8,128)S(1)}, u32[]{:S(2)}, u32[]{:S(2)}) collective-permute-start(f32[16,768]{1,0:T(8,128)S(1)} %fusion), channel_id=1, source_target_pairs={{0,4},{1,5},{2,6},{3,7},{4,8},{5,9},{6,10},{7,11},{8,12},{9,13},{1... | collective-permute-start | bytes 147464
  250.8 2.8 collective-permute-done.7
  253.6 7.7 %collective-permute-start.4 = (f32[16,768]{1,0:T(8,128)S(1)}, f32[16,768]{1,0:T(8,128)S(1)}, u32[]{:S(2)}, u32[]{:S(2)}) collective-permute-start(f32[16,768]{1,0:T(8,128)S(1)} %fusion), channel_id=1, source_target_pairs={{0,5},{1,6},{2,7},{3,8},{4,9},{5,10},{6,11},{7,12},{8,13},{9,14},{... | collective-permute-start | bytes 147464
  261.3 0.0 collective-permute-done
  261.3 1.9 collective-permute-start.5
  263.2 0.0 collective-permute-done.1
  263.3 1.9 collective-permute-start.6
  265.2 0.1 dynamic-slice.2
  265.3 1.3 dynamic-slice.5
  267.2 0.0 collective-permute-done.2
  267.2 0.0 collective-permute-done.3
  267.2 0.0 collective-permute-done.4
  267.2 1.0 collective-permute-done.5
  268.2 0.5 collective-permute-done.6
  268.7 1.0 concatenate.54
  269.8 0.9 copy.33
  270.7 0.0 reduce-scatter.6.cloned.1.call-update
  270.7 0.1 fusion.46
  270.9 0.7 copy.27
  271.6 104.0 %reduce-scatter.6.cloned.1.call-done = f32[48,12]{1,0:T(8,128)} async-done(((f32[768,12]{1,0:T(8,128)}), f32[48,12]{1,0:T(8,128)}) %reduce-scatter.6.cloned.1.call-update) | async-done | bytes 2320
  375.6 0.8 copy.34
  376.4 0.6 copy.28
  (5 shorter events, 0.1 us)
Async XLA Ops:
  7.2 12.9 %copy-start = (bf16[1,256,384]{2,1,0:T(8,128)(2,1)S(1)}, bf16[1,256,384]{2,1,0:T(8,128)(2,1)}, u32[]{:S(2)}) copy-start(bf16[1,256,384]{2,1,0:T(8,128)(2,1)} %param.11) | copy-start | bytes 589828
  7.2 5.6 %copy-start.1 = (bf16[1,384,768]{2,1,0:T(8,128)(2,1)S(1)}, bf16[1,384,768]{2,1,0:T(8,128)(2,1)}, u32[]{:S(2)}) copy-start(bf16[1,384,768]{2,1,0:T(8,128)(2,1)} %param.8) | copy-start | bytes 1769476
  7.2 155.3 %all-gather.2.cloned.1.call-start = ((), (), s32[]{:S(2)}) async-start(), calls=%async_computation.1 | async-start | bytes 4456448 | tf_op jit(solution)/shard_map/all_gather | solution.py:87
  20.1 2.3 copy-start.2
  22.3 0.7 copy-start.5
  22.4 1.6 copy-start.4
  23.9 351.7 %reduce-scatter.6.cloned.1.call-start = ((), (), s32[]{:S(2)}) async-start(), calls=%async_computation.2 | async-start | bytes 417792
  166.6 1.0 copy-start.3
  234.9 26.4 %collective-permute-start = (f32[16,768]{1,0:T(8,128)S(1)}, f32[16,768]{1,0:T(8,128)S(1)}, u32[]{:S(2)}, u32[]{:S(2)}) collective-permute-start(f32[16,768]{1,0:T(8,128)S(1)} %fusion), channel_id=1, source_target_pairs={{0,1},{1,2},{2,3},{3,4},{4,5},{5,6},{6,7},{7,8},{8,9},{9,10},{10,1... | collective-permute-start | bytes 147464
  236.8 26.4 %collective-permute-start.1 = (f32[16,768]{1,0:T(8,128)S(1)}, f32[16,768]{1,0:T(8,128)S(1)}, u32[]{:S(2)}, u32[]{:S(2)}) collective-permute-start(f32[16,768]{1,0:T(8,128)S(1)} %fusion), channel_id=1, source_target_pairs={{0,2},{1,3},{2,4},{3,5},{4,6},{5,7},{6,8},{7,9},{8,10},{9,11},{10,... | collective-permute-start | bytes 147464
  238.7 14.9 %collective-permute-start.7 = (f32[12,768]{1,0:T(8,128)S(1)}, f32[12,768]{1,0:T(8,128)S(1)}, u32[]{:S(2)}, u32[]{:S(2)}) collective-permute-start(f32[12,768]{1,0:T(8,128)S(1)} %slice.82), channel_id=1, source_target_pairs={{0,8},{1,9},{2,10},{3,11},{4,12},{5,13},{6,14},{7,15},{8,16},{9,17... | collective-permute-start | bytes 110600
  242.2 25.0 %collective-permute-start.2 = (f32[16,768]{1,0:T(8,128)S(1)}, f32[16,768]{1,0:T(8,128)S(1)}, u32[]{:S(2)}, u32[]{:S(2)}) collective-permute-start(f32[16,768]{1,0:T(8,128)S(1)} %fusion), channel_id=1, source_target_pairs={{0,3},{1,4},{2,5},{3,6},{4,7},{5,8},{6,9},{7,10},{8,11},{9,12},{10... | collective-permute-start | bytes 147464
  244.1 23.1 %collective-permute-start.3 = (f32[16,768]{1,0:T(8,128)S(1)}, f32[16,768]{1,0:T(8,128)S(1)}, u32[]{:S(2)}, u32[]{:S(2)}) collective-permute-start(f32[16,768]{1,0:T(8,128)S(1)} %fusion), channel_id=1, source_target_pairs={{0,4},{1,5},{2,6},{3,7},{4,8},{5,9},{6,10},{7,11},{8,12},{9,13},{1... | collective-permute-start | bytes 147464
  253.6 13.6 %collective-permute-start.4 = (f32[16,768]{1,0:T(8,128)S(1)}, f32[16,768]{1,0:T(8,128)S(1)}, u32[]{:S(2)}, u32[]{:S(2)}) collective-permute-start(f32[16,768]{1,0:T(8,128)S(1)} %fusion), channel_id=1, source_target_pairs={{0,5},{1,6},{2,7},{3,8},{4,9},{5,10},{6,11},{7,12},{8,13},{9,14},{... | collective-permute-start | bytes 147464
  261.3 6.9 %collective-permute-start.5 = (f32[16,768]{1,0:T(8,128)S(1)}, f32[16,768]{1,0:T(8,128)S(1)}, u32[]{:S(2)}, u32[]{:S(2)}) collective-permute-start(f32[16,768]{1,0:T(8,128)S(1)} %fusion), channel_id=1, source_target_pairs={{0,6},{1,7},{2,8},{3,9},{4,10},{5,11},{6,12},{7,13},{8,14},{9,15},... | collective-permute-start | bytes 147464
  263.3 5.5 %collective-permute-start.6 = (f32[16,768]{1,0:T(8,128)S(1)}, f32[16,768]{1,0:T(8,128)S(1)}, u32[]{:S(2)}, u32[]{:S(2)}) collective-permute-start(f32[16,768]{1,0:T(8,128)S(1)} %fusion), channel_id=1, source_target_pairs={{0,7},{1,8},{2,9},{3,10},{4,11},{5,12},{6,13},{7,14},{8,15},{9,16}... | collective-permute-start | bytes 147464
Sparse Core Ops, SparseCore 0:
  24.0 138.5 all-gather.1
  270.9 104.6 reduce-scatter.5
